TPU v7x, 32 devices: a whole 2x2x4 slice. The times are simulated.
32 devices in a mesh: groups: 2 (over y), replica: 4 (over z), sx: 4 (over x, core).
Axes of the slice: x: 2, y: 2, z: 4, core: 2. Of those that a mesh axis runs over, the one named last changes fastest.
Arguments:
- coords: float32 [3, 8, 4096], P(None, ('groups', 'replica'), 'sx'), parts along dimension 1, may hold values from 0 to 1
- widths: float32 [8, 4096], P(('groups', 'replica'), 'sx'), parts along dimension 0, may hold values from 1 to 2
- amplitudes: float32 [8, 4096], P(('groups', 'replica'), 'sx'), parts along dimension 0, may hold values from 1 to 4
- live_blocks: int32 [8, 4], P(('groups', 'replica'), 'sx'), parts along dimension 0, may hold values from 1 to 8, as said below
- target_map: float32 [192, 64, 480], P(('groups', 'sx')), parts along dimension 0, may hold values from -2 to 2
Outputs:
- mean_density: float32 [192, 64, 480], P(('groups', 'sx'), 'replica'), parts along dimension 0
- forces: float32 [3, 8, 4096], P(None, ('groups', 'replica'), 'sx'), parts along dimension 1
There are 2 independent parts, one for each index of `groups`. A program takes and returns all parts, laid end to end along the dimension named above; each array names one. Nothing has to cross between parts.
Inputs may be any that keep to these rules, and one draw needn't show every extreme that they name: `live_blocks`: blocks past the count hold padding slots. Some member's brick has all 8 blocks in use in every draw.
All inputs are finite; a program needn't handle non-finite values.
Results may differ from a plain program's by a relative error of at most 0.0044.
Values may be sent and summed in bfloat16 or wider, within the bound.
No kernel may reach another device: no remote copies, remote signals or barrier semaphores. Data moves between devices by JAX's collectives and lax.ppermute only.
A program may use at most 64 MiB of HBM per device.

v0:
```python
import functools
import math

import jax
import jax.numpy as jnp
from jax import lax
from jax.experimental import pallas as pl
from jax.experimental.pallas import tpu as pltpu
from jax.sharding import PartitionSpec as P

CX = 24
NZ = 64
NY = 480
REACH = 6
BLOCK = 128
BLOCKS = 8
ATOMS_DEV = 1024
SPAN = CX + 2 * REACH
LAP = 2 * REACH
LANES = 512
FIELDS = 5
HALF_LOG2E = 0.5 * math.log2(math.e)
STASH_LIMIT = 4

noise_floor = 0.05


def pack_kernel(
    zs, sliced, coords_ref, widths_ref, amplitudes_ref, live_ref, target_ref,
    own_ref, first_ref, second_ref, sems,
):
    odd = lax.rem(lax.axis_index("sx"), 2)
    planes = (CX - REACH) * (1 - odd), (CX - REACH) * odd
    copies = []
    for k, (plane, out) in enumerate(zip(planes, (first_ref, second_ref))):
        if sliced:
            z_first = pl.multiple_of(lax.axis_index("replica") * zs, 8)
            source = target_ref.at[pl.ds(plane, REACH), pl.ds(z_first, zs), :]
        else:
            source = target_ref.at[pl.ds(plane, REACH)]
        copies.append(pltpu.make_async_copy(source, out, sems.at[k]))
        copies[-1].start()
    block = lax.broadcasted_iota(jnp.int32, (BLOCKS, BLOCK), 0)
    own_ref[0:3] = coords_ref[...]
    own_ref[3] = widths_ref[...]
    own_ref[4] = jnp.where(block < live_ref[0, 0], amplitudes_ref[...], 0.0)
    for copy in copies:
        copy.wait()


def refine_kernel(
    members, zp, zs, sliced, stash, atoms_ref, near_ref, far_ref, near_target, far_target,
    target_ref, mean_ref, *rest,
):
    outs = rest[: len(rest) - 13]
    (rho, grad, wanted, mean_vmem, gy, gy_side, left, left_side, pulled, rows, forces, order, sems) = rest[
        len(outs) :
    ]
    rank = lax.axis_index("replica")
    brick = lax.axis_index("sx")
    last_plane = CX * lax.axis_size("sx")
    odd = lax.rem(brick, 2)
    slots = members * BLOCKS

    if sliced:
        z_first = rank * zs
        source = target_ref.at[:, pl.ds(pl.multiple_of(z_first, 8), zs), :]
    else:
        z_first = rank * zs
        source = target_ref
    fetches = [
        pltpu.make_async_copy(source, wanted.at[pl.ds(REACH, CX)], sems.at[0]),
        pltpu.make_async_copy(
            near_target, wanted.at[pl.ds((REACH + CX) * (1 - odd), REACH)], sems.at[1]
        ),
        pltpu.make_async_copy(far_target, wanted.at[pl.ds((REACH + CX) * odd, REACH)], sems.at[2]),
    ]
    for fetch in fetches:
        fetch.start()

    block_number = (lax.broadcasted_iota(jnp.int32, (BLOCKS, BLOCK), 0) + 1).astype(jnp.float32)

    def live_of(ref, member):
        return jnp.max(jnp.where(ref[member, 4] != 0.0, block_number, 0.0)).astype(jnp.int32)

    def listed(ref, start, base, filled):
        def one_member(member, count):
            def one(block, inner):
                order[inner] = base + member * BLOCKS + block
                return inner + 1

            return lax.fori_loop(start, live_of(ref, member), one, count)

        return lax.fori_loop(0, members, one_member, filled, unroll=members <= 4)

    def first_block(member, carry):
        order[member] = member * BLOCKS
        return carry

    lax.fori_loop(0, members, first_block, 0)
    own_count = listed(atoms_ref, 1, 0, members)
    side_first = slots
    side_near = listed(near_ref, 0, 0, side_first)
    side_count = listed(far_ref, 0, slots, side_near) - side_first

    forces[...] = jnp.zeros_like(forces)
    grad[:, :, NY - 96 :] = jnp.zeros((members, SPAN * zp, LANES - NY + 96), jnp.bfloat16)
    for k in range(gy.shape[0]):
        gy[k, NY:, :] = jnp.zeros((LANES - NY, 2 * BLOCK), jnp.bfloat16)
    for k in range(2):
        gy_side[k, NY:, :] = jnp.zeros((LANES - NY, BLOCK), jnp.bfloat16)

    step = lax.broadcasted_iota(jnp.int32, (16, BLOCK), 0).astype(jnp.float32)
    step_z = lax.broadcasted_iota(jnp.int32, (zp, BLOCK), 0)
    own_z = (step_z < zs).astype(jnp.float32)
    cell_z = (step_z + z_first).astype(jnp.float32)

    def fields(ref, member, block):
        data = [ref[member, f, pl.ds(block, 1), :] for f in range(FIELDS)]
        inv = 1.0 / data[3]
        q = inv * inv
        return data[0], data[1], data[2], q, q * -HALF_LOG2E, data[4]

    def table_y(out, frac, power, q, slopes):
        base = step - NY * frac
        for k in range(NY // 16):
            off = base + float(16 * k)
            value = jnp.exp2(off * off * power)
            out[16 * k : 16 * k + 16, 0:BLOCK] = value.astype(jnp.bfloat16)
            if slopes:
                out[16 * k : 16 * k + 16, BLOCK:] = (value * (off * q)).astype(jnp.bfloat16)

    def table_x(frac, power, shift, lower, count, edges):
        cell = lax.broadcasted_iota(jnp.int32, (count, BLOCK), 0) + lower
        off = cell.astype(jnp.float32) - (CX * frac + shift)
        value = jnp.exp2(off * off * power)
        if edges:
            plane = cell + (brick * CX - REACH)
            value = jnp.where((plane >= 0) & (plane < last_plane), value, 0.0)
        return value, off

    def table_z(frac, power):
        off = cell_z - NZ * frac
        value = jnp.exp2(off * off * power)
        return (value if zs == zp else value * own_z), off

    def fill_left(out, scaled, gz, count, part):
        rows[part, 0:count] = scaled
        group = max(1, 16 // zp)
        for t in range(0, count, group):
            pieces = [rows[part, t + i : t + i + 1] * gz for i in range(group)]
            piece = pieces[0] if group == 1 else jnp.concatenate(pieces, 0)
            out[t * zp : (t + group) * zp] = piece.astype(jnp.bfloat16)

    def matmul_t(a, b):
        return lax.dot_general(a, b, (((1,), (1,)), ((), ())), preferred_element_type=jnp.float32)

    def own_splat(unit, slot, part, keep, fresh):
        code = order[unit]
        member, block = code // BLOCKS, lax.rem(code, BLOCKS)
        frac_x, frac_y, frac_z, q, power, weight = fields(atoms_ref, member, block)
        gx, _ = table_x(frac_x, power, REACH, 0, SPAN, True)
        gz, _ = table_z(frac_z, power)
        table_y(gy.at[slot], frac_y, power, q, stash)
        fill_left(left.at[part], weight * keep * gx, gz, SPAN, part)
        add = matmul_t(left[part], gy[slot, :, 0:BLOCK])
        return member, add

    def start_members(pair, carry):
        for part in range(2):
            unit = 2 * pair + part
            member, add = own_splat(unit, unit if stash else part, part, 1.0, True)
            rho[member] = add
        return carry

    lax.fori_loop(0, members // 2, start_members, 0)

    def more_blocks(pair, carry):
        done = []
        for part in range(2):
            unit = members + 2 * pair + part
            keep = jnp.where(unit < own_count, 1.0, 0.0)
            at = jnp.minimum(unit, own_count - 1)
            done.append(own_splat(at, at if stash else part, part, keep, False))
        for member, add in done:
            rho[member] += add
        return carry

    lax.fori_loop(0, (own_count - members + 1) // 2, more_blocks, 0)

    def side_blocks(ref, base, above):
        lower = CX * above
        shift = REACH - CX + 2 * CX * above

        def one_pair(pair, carry):
            done = []
            for part in range(2):
                unit = 2 * pair + part
                keep = jnp.where(unit < base[1], 1.0, 0.0)
                code = order[side_first + jnp.minimum(unit, base[1] - 1)] - base[2]
                member, block = code // BLOCKS, lax.rem(code, BLOCKS)
                frac_x, frac_y, frac_z, q, power, weight = fields(ref, member, block)
                gx, _ = table_x(
                    frac_x, power, shift.astype(jnp.float32), lower, LAP, False
                )
                gz, _ = table_z(frac_z, power)
                table_y(gy_side.at[part], frac_y, power, q, False)
                fill_left(left_side.at[part], weight * keep * gx, gz, LAP, part)
                done.append((member, matmul_t(left_side[part], gy_side[part])))
            for member, add in done:
                at = pl.ds(pl.multiple_of(lower * zp, 16), LAP * zp)
                rho[member, at, :] += add
            return carry

        lax.fori_loop(base[0] // 2, (base[1] + 1) // 2, one_pair, 0)

    near_count = side_near - side_first
    side_blocks(near_ref, (0, near_count, 0), 1 - odd)
    side_first = side_near
    side_blocks(far_ref, (0, side_count - near_count, slots), odd)

    for fetch in fetches:
        fetch.wait()

    group = max(1, 16 // zp)

    def gradient(t, carry):
        at = pl.ds(pl.multiple_of(t * group * zp, 16), group * zp)
        planes = pl.ds(t * group, group)
        here = [rho[m, at, 0:NY] for m in range(members)]
        first = functools.reduce(jnp.add, here)
        second = functools.reduce(jnp.add, [f * f for f in here])
        mean = first * (1.0 / members)
        spread = second * (1.0 / members) - mean * mean
        inv = 1.0 / (noise_floor + spread * (1.0 / members))
        pull = (wanted[planes].reshape(group * zp, NY) - mean) * inv
        gain = (inv - pull * pull) * (1.0 / (members * members))
        offset = pull * (-1.0 / members) - gain * mean
        for m in range(members):
            grad[m, at, 0:NY] = (offset + gain * here[m]).astype(jnp.bfloat16)
        mean_vmem[planes] = mean.reshape(group, zp, NY)
        return carry

    lax.fori_loop(0, SPAN // group, gradient, 0)
    give = pltpu.make_async_copy(mean_vmem.at[pl.ds(REACH, CX)], mean_ref, sems.at[3])
    give.start()

    def pull_pair(pair, carry):
        for part in range(2):
            unit = jnp.minimum(2 * pair + part, own_count - 1)
            code = order[unit]
            member, block = code // BLOCKS, lax.rem(code, BLOCKS)
            frac_x, frac_y, frac_z, q, power, weight = fields(atoms_ref, member, block)
            gx, off_x = table_x(frac_x, power, REACH, 0, SPAN, True)
            gz, off_z = table_z(frac_z, power)
            rows[part, 0:SPAN] = gx
            rows[part, SPAN : 2 * SPAN] = gx * off_x * q
            slot = unit if stash else part
            if not stash:
                table_y(gy.at[slot], frac_y, power, q, True)
            pulled[part] = jnp.dot(grad[member], gy[slot], preferred_element_type=jnp.float32)
            sum_x = jnp.zeros((zp, BLOCK), jnp.float32)
            sum_y = jnp.zeros((zp, BLOCK), jnp.float32)
            sum_z = jnp.zeros((zp, BLOCK), jnp.float32)
            for t in range(SPAN):
                plain = pulled[part, t * zp : (t + 1) * zp, 0:BLOCK]
                slanted = pulled[part, t * zp : (t + 1) * zp, BLOCK:]
                here = rows[part, t : t + 1]
                sum_x += rows[part, SPAN + t : SPAN + t + 1] * plain
                sum_y += here * slanted
                sum_z += here * plain
            at = pl.ds(block, 1)
            forces[member, 0, at] = weight * jnp.sum(sum_x * gz, 0, keepdims=True)
            forces[member, 1, at] = weight * jnp.sum(sum_y * gz, 0, keepdims=True)
            forces[member, 2, at] = weight * jnp.sum(sum_z * (gz * off_z * q), 0, keepdims=True)
        return carry

    lax.fori_loop(0, (own_count + 1) // 2, pull_pair, 0)
    if len(outs) == 1:
        outs[0][...] = forces[...]
    else:
        for m, out in enumerate(outs):
            out[...] = forces[m]
    give.wait()


def shards(coords, widths, amplitudes, live_blocks, target_map):
    members = lax.axis_size("replica")
    bricks = lax.axis_size("sx")
    rank = lax.axis_index("replica")
    zs = NZ // members
    zp = max(zs, 8)
    sliced = zs % 8 == 0
    few = members <= 4 and members & (members - 1) == 0
    stash = members <= STASH_LIMIT
    blocks = (BLOCKS, BLOCK)
    vmem = pl.BlockSpec(memory_space=pltpu.VMEM)
    smem = pl.BlockSpec(memory_space=pltpu.SMEM)
    anywhere = pl.BlockSpec(memory_space=pl.ANY)

    target = target_map
    if not sliced:
        part = lax.dynamic_slice_in_dim(target_map, rank * zs, zs, 1)
        target = jnp.pad(part, ((0, 0), (0, zp - zs), (0, 0)))
    edge = jax.ShapeDtypeStruct((REACH, zp, NY), jnp.float32)
    own, near_edge, far_edge = pl.pallas_call(
        functools.partial(pack_kernel, zs, sliced),
        out_shape=(jax.ShapeDtypeStruct((FIELDS,) + blocks, jnp.float32), edge, edge),
        in_specs=[vmem, vmem, vmem, smem, anywhere],
        out_specs=(vmem, vmem, vmem),
        scratch_shapes=[pltpu.SemaphoreType.DMA((2,))],
        name="pack",
    )(coords.reshape((3,) + blocks), widths.reshape(blocks), amplitudes.reshape(blocks), live_blocks, target)

    def swap(block, pairs):
        return lax.ppermute(block, "sx", pairs + [(b, a) for a, b in pairs])

    near_pairs = [(i, i + 1) for i in range(0, bricks - 1, 2)]
    far_pairs = [(i, i + 1) for i in range(1, bricks - 1, 2)]

    def across(block, k):
        return lax.ppermute(block, "replica", [(i, i ^ k) for i in range(members)])

    if few:
        everyone = jnp.stack([own] + [across(own, k) for k in range(1, members)])
    else:
        everyone = lax.all_gather(own, "replica")
    near_target, far_target = swap(near_edge, near_pairs), swap(far_edge, far_pairs)
    far, near = swap(everyone, far_pairs), swap(everyone, near_pairs)

    force_shapes = (
        [jax.ShapeDtypeStruct((3,) + blocks, jnp.float32)] * members
        if few
        else [jax.ShapeDtypeStruct((members, 3) + blocks, jnp.float32)]
    )
    slots = members * BLOCKS if stash else 2
    mean, *partial = pl.pallas_call(
        functools.partial(refine_kernel, members, zp, zs, sliced, stash),
        out_shape=[jax.ShapeDtypeStruct((CX, zp, NY), jnp.float32)] + force_shapes,
        in_specs=[vmem, vmem, vmem, anywhere, anywhere, anywhere],
        out_specs=[anywhere] + [vmem] * len(force_shapes),
        scratch_shapes=[
            pltpu.VMEM((members, SPAN * zp, LANES), jnp.float32),
            pltpu.VMEM((members, SPAN * zp, LANES), jnp.bfloat16),
            pltpu.VMEM((SPAN, zp, NY), jnp.float32),
            pltpu.VMEM((SPAN, zp, NY), jnp.float32),
            pltpu.VMEM((slots, LANES, 2 * BLOCK), jnp.bfloat16),
            pltpu.VMEM((2, LANES, BLOCK), jnp.bfloat16),
            pltpu.VMEM((2, SPAN * zp, BLOCK), jnp.bfloat16),
            pltpu.VMEM((2, LAP * zp, BLOCK), jnp.bfloat16),
            pltpu.VMEM((2, SPAN * zp, 2 * BLOCK), jnp.float32),
            pltpu.VMEM((2, 2 * SPAN, BLOCK), jnp.float32),
            pltpu.VMEM((members, 3) + blocks, jnp.float32),
            pltpu.SMEM((3 * members * BLOCKS + 1,), jnp.int32),
            pltpu.SemaphoreType.DMA((4,)),
        ],
        compiler_params=pltpu.CompilerParams(vmem_limit_bytes=44 * 1024 * 1024),
        name="refine",
    )(everyone, near, far, near_target, far_target, target)

    if few:
        forces = partial[0]
        for k in range(1, members):
            forces = forces + across(partial[k], k)
    else:
        forces = lax.psum_scatter(partial[0], "replica", scatter_dimension=0)
    return mean[:, :zs], forces.reshape(3, 1, ATOMS_DEV)


def solution(mesh):
    placed = (
        P(None, ("groups", "replica"), "sx"),
        P(("groups", "replica"), "sx"),
        P(("groups", "replica"), "sx"),
        P(("groups", "replica"), "sx"),
        P(("groups", "sx"), None, None),
    )
    return jax.shard_map(
        shards,
        mesh=mesh,
        in_specs=placed,
        out_specs=(P(("groups", "sx"), "replica", None), P(None, ("groups", "replica"), "sx")),
        check_vma=False,
    )
```

profile of v0, /device:TPU:1, one launch (start us, length us, event | category | flops | bytes accessed | tf_op | source)
XLA Modules:
  0.0 45.8 jit_solution(13062466710440303848)
XLA Ops:
  0.6 0.0 copy-start
  1.4 2.7 %pack.1 = (f32[5,8,128]{2,1,0:T(8,128)}, f32[6,16,480]{2,1,0:T(8,128)}, f32[6,16,480]{2,1,0:T(8,128)}) custom-call(f32[3,8,128]{2,1,0:T(8,128)} %bitcast.12, f32[8,128]{1,0:T(8,128)} %bitcast.14, f32[8,128]{1,0:T(8,128)} %bitcast.15, s32[1,1]{1,0:T(1,128)S(6)} %copy.9.live_ref, f32[24,64,480]{2,1,0:T(8,128)} %target_ref.3), custom_call_target="tpu_custom_call" | custom-call | tf_op jit(solution)/shard_map/pack/pallas_call | solution.py:306
  4.1 4.2 %collective-permute-start.2 = (f32[5,8,128]{2,1,0:T(8,128)}, f32[5,8,128]{2,1,0:T(8,128)S(1)}, u32[]{:S(2)}, u32[]{:S(2)}) collective-permute-start(f32[5,8,128]{2,1,0:T(8,128)} %get-tuple-element.10), channel_id=1, source_target_pairs={{0,12},{4,8},{8,4},{12,0},{1,13},{5,9},{9,5},{13,1},{2,14},{6,10},... | collective-permute-start | bytes 61448 | tf_op jit(solution)/shard_map/ppermute | solution.py:322
  8.3 0.0 collective-permute-start.1
  8.3 0.4 collective-permute-start
  8.7 1.2 %collective-permute-start.5 = (f32[6,16,480]{2,1,0:T(8,128)}, f32[6,16,480]{2,1,0:T(8,128)S(1)}, u32[]{:S(2)}, u32[]{:S(2)}) collective-permute-start(f32[6,16,480]{2,1,0:T(8,128)} %get-tuple-element.11), channel_id=1, source_target_pairs={{0,1},{2,3},{1,0},{3,2},{4,5},{6,7},{5,4},{7,6},{8,9},{10,11},{9,8... | collective-permute-start | bytes 552968 | tf_op jit(solution)/shard_map/ppermute | solution.py:316
  9.9 3.1 %collective-permute-start.6 = (f32[6,16,480]{2,1,0:T(8,128)}, f32[6,16,480]{2,1,0:T(8,128)S(1)}, u32[]{:S(2)}, u32[]{:S(2)}) collective-permute-start(f32[6,16,480]{2,1,0:T(8,128)} %get-tuple-element.12), channel_id=1, source_target_pairs={{1,2},{2,1},{5,6},{6,5},{9,10},{10,9},{13,14},{14,13},{17,18},{18,... | collective-permute-start | bytes 552968 | tf_op jit(solution)/shard_map/ppermute | solution.py:316
  13.1 0.0 collective-permute-done.2
  13.1 0.0 collective-permute-done.1
  13.1 0.0 collective-permute-done
  13.1 0.7 %pad_maximum_fusion.atoms_ref = f32[4,5,8,128]{3,2,1,0:T(8,128)S(1)} fusion(f32[1,5,8,128]{3,2,1,0:T(8,128)S(1)} %bitcast.9, f32[1,5,8,128]{3,2,1,0:T(8,128)S(1)} %bitcast.10, f32[1,5,8,128]{3,2,1,0:T(8,128)S(1)} %bitcast.11, f32[1,5,8,128]{3,2,1,0:T(8,128)} %bitcast.8), kind=kLoop, calls=%fused_computation | loop fusion | flops 61440 | bytes 163840 | tf_op jit(solution)/shard_map/stack | solution.py:325
  13.8 4.1 %collective-permute-start.4 = (f32[4,5,8,128]{3,2,1,0:T(8,128)S(1)}, f32[4,5,8,128]{3,2,1,0:T(8,128)S(1)}, u32[]{:S(2)}, u32[]{:S(2)}) collective-permute-start(f32[4,5,8,128]{3,2,1,0:T(8,128)S(1)} %pad_maximum_fusion.atoms_ref), channel_id=1, source_target_pairs={{1,2},{2,1},{5,6},{6,5},{9,10},{10,9},{13,14},{14,13},{17,18},{18,... | collective-permute-start | bytes 245768 | tf_op jit(solution)/shard_map/ppermute | solution.py:316
  17.9 0.1 collective-permute-start.3
  18.0 2.0 %collective-permute-done.4.far_ref = f32[4,5,8,128]{3,2,1,0:T(8,128)S(1)} collective-permute-done((f32[4,5,8,128]{3,2,1,0:T(8,128)S(1)}, f32[4,5,8,128]{3,2,1,0:T(8,128)S(1)}, u32[]{:S(2)}, u32[]{:S(2)}) %collective-permute-start.4) | collective-permute-done | bytes 81952 | tf_op jit(solution)/shard_map/ppermute | solution.py:316
  20.0 0.0 collective-permute-done.3.near_ref
  20.0 0.0 collective-permute-done.5.near_target
  20.0 0.0 collective-permute-done.6.far_target
  20.0 0.0 copy-done
  20.1 17.6 %refine.1 = (f32[24,16,480]{2,1,0:T(8,128)}, f32[3,8,128]{2,1,0:T(8,128)S(1)}, f32[3,8,128]{2,1,0:T(8,128)S(1)}, f32[3,8,128]{2,1,0:T(8,128)S(1)}, f32[3,8,128]{2,1,0:T(8,128)S(1)}) custom-call(f32[4,5,8,128]{3,2,1,0:T(8,128)S(1)} %pad_maximum_fusion.atoms_ref, f32[4,5,8,128]{3,2,1,0:T(8,128)S(1)} %collective-permute-done.3.near_ref, ...), custom_call_target="tpu_custom_call" | custom-call | tf_op jit(solution)/shard_map/refine/pallas_call | solution.py:337
  37.6 0.6 %collective-permute-start.7 = (f32[3,8,128]{2,1,0:T(8,128)S(1)}, f32[3,8,128]{2,1,0:T(8,128)S(1)}, u32[]{:S(2)}, u32[]{:S(2)}) collective-permute-start(f32[3,8,128]{2,1,0:T(8,128)S(1)} %get-tuple-element.15), channel_id=1, source_target_pairs={{0,4},{4,0},{8,12},{12,8},{1,5},{5,1},{9,13},{13,9},{2,6},{6,2},{1... | collective-permute-start | bytes 36872 | tf_op jit(solution)/shard_map/ppermute | solution.py:322
  38.2 2.6 %collective-permute-start.8 = (f32[3,8,128]{2,1,0:T(8,128)S(1)}, f32[3,8,128]{2,1,0:T(8,128)S(1)}, u32[]{:S(2)}, u32[]{:S(2)}) collective-permute-start(f32[3,8,128]{2,1,0:T(8,128)S(1)} %get-tuple-element.16), channel_id=1, source_target_pairs={{0,8},{4,12},{8,0},{12,4},{1,9},{5,13},{9,1},{13,5},{2,10},{6,14},... | collective-permute-start | bytes 36872 | tf_op jit(solution)/shard_map/ppermute | solution.py:322
  40.8 0.4 collective-permute-start.9
  41.2 0.0 collective-permute-done.7
  41.2 0.7 %collective-permute-done.8 = f32[3,8,128]{2,1,0:T(8,128)S(1)} collective-permute-done((f32[3,8,128]{2,1,0:T(8,128)S(1)}, f32[3,8,128]{2,1,0:T(8,128)S(1)}, u32[]{:S(2)}, u32[]{:S(2)}) %collective-permute-start.8) | collective-permute-done | bytes 12320 | tf_op jit(solution)/shard_map/ppermute | solution.py:322
  41.9 3.3 %collective-permute-done.9 = f32[3,8,128]{2,1,0:T(8,128)S(1)} collective-permute-done((f32[3,8,128]{2,1,0:T(8,128)S(1)}, f32[3,8,128]{2,1,0:T(8,128)S(1)}, u32[]{:S(2)}, u32[]{:S(2)}) %collective-permute-start.9) | collective-permute-done | bytes 12320 | tf_op jit(solution)/shard_map/ppermute | solution.py:322
  45.2 0.6 %add_add_fusion = f32[3,8,128]{2,1,0:T(8,128)} fusion(f32[3,8,128]{2,1,0:T(8,128)S(1)} %collective-permute-done.9, f32[3,8,128]{2,1,0:T(8,128)S(1)} %collective-permute-done.8, f32[3,8,128]{2,1,0:T(8,128)S(1)} %get-tuple-element.14, f32[3,8,128]{2,1,0:T(8,128)S(1)} %collective-permute-done.7), kind=kLoop, calls=%fused_computation.1 | loop fusion | flops 9216 | bytes 61440 | tf_op jit(solution)/shard_map/add | solution.py:364
Async XLA Ops:
  0.6 19.4 %copy-start = (f32[24,64,480]{2,1,0:T(8,128)S(1)}, f32[24,64,480]{2,1,0:T(8,128)}, u32[]{:S(2)}) copy-start(f32[24,64,480]{2,1,0:T(8,128)} %target_ref.3) | copy-start | bytes 8847364
  4.1 9.0 %collective-permute-start.2 = (f32[5,8,128]{2,1,0:T(8,128)}, f32[5,8,128]{2,1,0:T(8,128)S(1)}, u32[]{:S(2)}, u32[]{:S(2)}) collective-permute-start(f32[5,8,128]{2,1,0:T(8,128)} %get-tuple-element.10), channel_id=1, source_target_pairs={{0,12},{4,8},{8,4},{12,0},{1,13},{5,9},{9,5},{13,1},{2,14},{6,10},... | collective-permute-start | bytes 61448 | tf_op jit(solution)/shard_map/ppermute | solution.py:322
  8.3 4.8 %collective-permute-start.1 = (f32[5,8,128]{2,1,0:T(8,128)}, f32[5,8,128]{2,1,0:T(8,128)S(1)}, u32[]{:S(2)}, u32[]{:S(2)}) collective-permute-start(f32[5,8,128]{2,1,0:T(8,128)} %get-tuple-element.10), channel_id=1, source_target_pairs={{0,8},{4,12},{8,0},{12,4},{1,9},{5,13},{9,1},{13,5},{2,10},{6,14},... | collective-permute-start | bytes 61448 | tf_op jit(solution)/shard_map/ppermute | solution.py:322
  8.3 4.8 %collective-permute-start = (f32[5,8,128]{2,1,0:T(8,128)}, f32[5,8,128]{2,1,0:T(8,128)S(1)}, u32[]{:S(2)}, u32[]{:S(2)}) collective-permute-start(f32[5,8,128]{2,1,0:T(8,128)} %get-tuple-element.10), channel_id=1, source_target_pairs={{0,4},{4,0},{8,12},{12,8},{1,5},{5,1},{9,13},{13,9},{2,6},{6,2},{1... | collective-permute-start | bytes 61448 | tf_op jit(solution)/shard_map/ppermute | solution.py:322
  8.7 11.3 %collective-permute-start.5 = (f32[6,16,480]{2,1,0:T(8,128)}, f32[6,16,480]{2,1,0:T(8,128)S(1)}, u32[]{:S(2)}, u32[]{:S(2)}) collective-permute-start(f32[6,16,480]{2,1,0:T(8,128)} %get-tuple-element.11), channel_id=1, source_target_pairs={{0,1},{2,3},{1,0},{3,2},{4,5},{6,7},{5,4},{7,6},{8,9},{10,11},{9,8... | collective-permute-start | bytes 552968 | tf_op jit(solution)/shard_map/ppermute | solution.py:316
  9.9 10.1 %collective-permute-start.6 = (f32[6,16,480]{2,1,0:T(8,128)}, f32[6,16,480]{2,1,0:T(8,128)S(1)}, u32[]{:S(2)}, u32[]{:S(2)}) collective-permute-start(f32[6,16,480]{2,1,0:T(8,128)} %get-tuple-element.12), channel_id=1, source_target_pairs={{1,2},{2,1},{5,6},{6,5},{9,10},{10,9},{13,14},{14,13},{17,18},{18,... | collective-permute-start | bytes 552968 | tf_op jit(solution)/shard_map/ppermute | solution.py:316
  13.8 6.2 %collective-permute-start.4 = (f32[4,5,8,128]{3,2,1,0:T(8,128)S(1)}, f32[4,5,8,128]{3,2,1,0:T(8,128)S(1)}, u32[]{:S(2)}, u32[]{:S(2)}) collective-permute-start(f32[4,5,8,128]{3,2,1,0:T(8,128)S(1)} %pad_maximum_fusion.atoms_ref), channel_id=1, source_target_pairs={{1,2},{2,1},{5,6},{6,5},{9,10},{10,9},{13,14},{14,13},{17,18},{18,... | collective-permute-start | bytes 245768 | tf_op jit(solution)/shard_map/ppermute | solution.py:316
  17.9 2.1 %collective-permute-start.3 = (f32[4,5,8,128]{3,2,1,0:T(8,128)S(1)}, f32[4,5,8,128]{3,2,1,0:T(8,128)S(1)}, u32[]{:S(2)}, u32[]{:S(2)}) collective-permute-start(f32[4,5,8,128]{3,2,1,0:T(8,128)S(1)} %pad_maximum_fusion.atoms_ref), channel_id=1, source_target_pairs={{0,1},{2,3},{1,0},{3,2},{4,5},{6,7},{5,4},{7,6},{8,9},{10,11},{9,8... | collective-permute-start | bytes 245768 | tf_op jit(solution)/shard_map/ppermute | solution.py:316
  37.6 3.6 %collective-permute-start.7 = (f32[3,8,128]{2,1,0:T(8,128)S(1)}, f32[3,8,128]{2,1,0:T(8,128)S(1)}, u32[]{:S(2)}, u32[]{:S(2)}) collective-permute-start(f32[3,8,128]{2,1,0:T(8,128)S(1)} %get-tuple-element.15), channel_id=1, source_target_pairs={{0,4},{4,0},{8,12},{12,8},{1,5},{5,1},{9,13},{13,9},{2,6},{6,2},{1... | collective-permute-start | bytes 36872 | tf_op jit(solution)/shard_map/ppermute | solution.py:322
  38.2 3.7 %collective-permute-start.8 = (f32[3,8,128]{2,1,0:T(8,128)S(1)}, f32[3,8,128]{2,1,0:T(8,128)S(1)}, u32[]{:S(2)}, u32[]{:S(2)}) collective-permute-start(f32[3,8,128]{2,1,0:T(8,128)S(1)} %get-tuple-element.16), channel_id=1, source_target_pairs={{0,8},{4,12},{8,0},{12,4},{1,9},{5,13},{9,1},{13,5},{2,10},{6,14},... | collective-permute-start | bytes 36872 | tf_op jit(solution)/shard_map/ppermute | solution.py:322
  40.8 4.3 %collective-permute-start.9 = (f32[3,8,128]{2,1,0:T(8,128)S(1)}, f32[3,8,128]{2,1,0:T(8,128)S(1)}, u32[]{:S(2)}, u32[]{:S(2)}) collective-permute-start(f32[3,8,128]{2,1,0:T(8,128)S(1)} %get-tuple-element.17), channel_id=1, source_target_pairs={{0,12},{4,8},{8,4},{12,0},{1,13},{5,9},{9,5},{13,1},{2,14},{6,10},... | collective-permute-start | bytes 36872 | tf_op jit(solution)/shard_map/ppermute | solution.py:322
where the time goes:
time: 45.9 us; the launch traced here: 45.8 us
  Pallas kernels  20.2 us (44%)
  starting transfers between devices  16.7 us (36%)
  waiting for transfers between devices  6 us (13%)
  between operations  1.52 us (3%)
  other arithmetic  1.34 us (3%)
    pallas_call x1, Pallas kernels, shards(): pl.pallas_call(functools.partial(refine_kernel, members, zp, zs, sliced,...  17.6 us
    ppermute x4, starting transfers between devices, swap(): return lax.ppermute(block, 'sx', pairs + [(b, a) for a, b in pairs])  8.51 us
    ppermute x6, starting transfers between devices, across(): return lax.ppermute(block, 'replica', [(i, i ^ k) for i in range(members)])  8.19 us
    ppermute x6, waiting for transfers between devices, across(): return lax.ppermute(block, 'replica', [(i, i ^ k) for i in range(members)])  3.97 us
    pallas_call x1, Pallas kernels, shards(): pl.pallas_call(functools.partial(pack_kernel, zs, sliced), out_shape=(jax...  2.67 us
    ppermute x4, waiting for transfers between devices, swap(): return lax.ppermute(block, 'sx', pairs + [(b, a) for a, b in pairs])  2.04 us
  transfers between devices with their start and end apart: 10, of which 3 were waited for; matrix products, arithmetic and copies ran while one was open for 2% of the time, Pallas kernels for 0%

commit v1 on v0

v1 whole, which is shorter than its diff:
```python
import functools
import math

import jax
import jax.numpy as jnp
from jax import lax
from jax.experimental import pallas as pl
from jax.experimental.pallas import tpu as pltpu
from jax.sharding import PartitionSpec as P

CX = 24
NZ = 64
NY = 480
REACH = 6
BLOCK = 128
BLOCKS = 8
ATOMS_DEV = 1024
SPAN = CX + 2 * REACH
LAP = 2 * REACH
LANES = 512
FIELDS = 5
HALF_LOG2E = 0.5 * math.log2(math.e)
STASH_LIMIT = 4

noise_floor = 0.05


def live_of(ref, member):
    number = (lax.broadcasted_iota(jnp.int32, (BLOCKS, BLOCK), 0) + 1).astype(jnp.float32)
    return jnp.max(jnp.where(ref[member, 4] != 0.0, number, 0.0)).astype(jnp.int32)


def listed(out, count, first, stride, base, live):
    for block in range(first, BLOCKS, stride):
        out[count] = base + block
        count = count + jnp.where(block < live, 1, 0)
    return count


class Tables:
    def __init__(self, zp, zs, atoms_ref):
        self.zp, self.zs, self.atoms_ref = zp, zs, atoms_ref
        self.brick = lax.axis_index("sx")
        self.last_plane = CX * lax.axis_size("sx")
        self.step = lax.broadcasted_iota(jnp.int32, (16, BLOCK), 0).astype(jnp.float32)
        step_z = lax.broadcasted_iota(jnp.int32, (zp, BLOCK), 0)
        self.own_z = (step_z < zs).astype(jnp.float32)
        self.cell_z = (step_z + lax.axis_index("replica") * zs).astype(jnp.float32)

    def fields(self, data):
        frac_x, frac_y, frac_z, width, weight = data
        inv = 1.0 / width
        q = inv * inv
        return frac_x, frac_y, frac_z, q, q * -HALF_LOG2E, weight

    def own_fields(self, member, block):
        return self.fields([self.atoms_ref[member, f, pl.ds(block, 1), :] for f in range(FIELDS)])

    def y(self, out, slopes, frac, power, q):
        base = self.step - NY * frac
        for k in range(NY // 16):
            off = base + float(16 * k)
            value = jnp.exp2(off * off * power)
            out[16 * k : 16 * k + 16, :] = value.astype(jnp.bfloat16)
            if slopes is not None:
                slopes[16 * k : 16 * k + 16, :] = (value * (off * q)).astype(jnp.bfloat16)

    def x(self, frac, power, shift, lower, count, edges):
        cell = lax.broadcasted_iota(jnp.int32, (count, BLOCK), 0) + lower
        off = cell.astype(jnp.float32) - (CX * frac + shift)
        value = jnp.exp2(off * off * power)
        if edges:
            plane = cell + (self.brick * CX - REACH)
            value = jnp.where((plane >= 0) & (plane < self.last_plane), value, 0.0)
        return value, off

    def z(self, frac, power):
        off = self.cell_z - NZ * frac
        value = jnp.exp2(off * off * power)
        return (value if self.zs == self.zp else value * self.own_z), off


def zero_tails(*tables):
    for table in tables:
        table[:, NY:, :] = jnp.zeros((table.shape[0], LANES - NY, BLOCK), jnp.bfloat16)


def splat_kernel(members, zp, zs, stash, atoms_ref, near_ref, far_ref, rho, *rest):
    if stash:
        gy, slope, gy_side, sides, left, left_side, rows, more_list, side_list = rest
    else:
        gy, gy_side, sides, left, left_side, rows, more_list, side_list = rest
        slope = None
    odd = lax.rem(lax.axis_index("sx"), 2)

    def list_member(member, counts):
        own, near, far = (live_of(ref, member) for ref in (atoms_ref, near_ref, far_ref))
        base = member * BLOCKS
        sides[0, member] = near_ref[member]
        sides[1, member] = far_ref[member]
        side_count = listed(side_list, counts[1], 0, 1, base, near)
        return (
            listed(more_list, counts[0], 2, 2, base, own),
            listed(side_list, side_count, 0, 1, members * BLOCKS + base, far),
        )

    more_count, side_count = lax.fori_loop(
        0, members, list_member, (jnp.int32(0),) * 2, unroll=members <= 4
    )
    zero_tails(gy, gy_side)
    if stash:
        zero_tails(slope)
    tables = Tables(zp, zs, atoms_ref)

    def fill_left(out, scaled, gz, count, here):
        here[0:count] = scaled
        group = max(1, 16 // zp)
        for t in range(0, count, group):
            pieces = [here[t + i : t + i + 1] * gz for i in range(group)]
            piece = pieces[0] if group == 1 else jnp.concatenate(pieces, 0)
            out[t * zp : (t + group) * zp] = piece.astype(jnp.bfloat16)

    def matmul_t(a, b):
        return lax.dot_general(a, b, (((1,), (1,)), ((), ())), preferred_element_type=jnp.float32)

    def own_splat(member, block, part):
        at = [member * BLOCKS + block + half if stash else 2 * part + half for half in range(2)]
        for half in range(2):
            spot = 2 * part + half
            frac_x, frac_y, frac_z, q, power, weight = tables.own_fields(member, block + half)
            gx, _ = tables.x(frac_x, power, REACH, 0, SPAN, True)
            gz, _ = tables.z(frac_z, power)
            tables.y(gy.at[at[half]], slope.at[at[half]] if stash else None, frac_y, power, q)
            fill_left(left.at[spot], weight * gx, gz, SPAN, rows.at[spot])
        return matmul_t(
            jnp.concatenate([left[2 * part], left[2 * part + 1]], 1),
            jnp.concatenate([gy[at[0]], gy[at[1]]], 1),
        )

    def start_members(pair, carry):
        for part in range(2):
            rho[2 * pair + part] = own_splat(2 * pair + part, 0, part)
        return carry

    lax.fori_loop(0, members // 2, start_members, 0)

    def more_blocks(unit, carry):
        code = more_list[unit]
        member, block = code // BLOCKS, lax.rem(code, BLOCKS)
        rho[member] += own_splat(member, block, 0)
        return carry

    lax.fori_loop(0, more_count, more_blocks, 0)

    side_group = gy_side.shape[0]

    def side_blocks(step_at, carry):
        done = []
        for part in range(side_group):
            unit = side_group * step_at + part
            code = side_list[jnp.minimum(unit, side_count - 1)]
            side, member = code // (members * BLOCKS), lax.rem(code // BLOCKS, members)
            above = jnp.where(side == 0, 1 - odd, odd)
            block = pl.ds(lax.rem(code, BLOCKS), 1)
            keep = jnp.where(unit < side_count, 1.0, 0.0)
            lower = CX * above
            shift = (REACH - CX + 2 * CX * above).astype(jnp.float32)
            frac_x, frac_y, frac_z, q, power, weight = tables.fields(
                [sides[side, member, f, block, :] for f in range(FIELDS)]
            )
            gx, _ = tables.x(frac_x, power, shift, lower, LAP, False)
            gz, _ = tables.z(frac_z, power)
            tables.y(gy_side.at[part], None, frac_y, power, q)
            fill_left(left_side.at[part], weight * keep * gx, gz, LAP, rows.at[part])
            at = pl.ds(pl.multiple_of(lower * zp, 16), LAP * zp)
            done.append((member, at, matmul_t(left_side[part], gy_side[part])))
        for member, at, add in done:
            rho[member, at, :] += add
        return carry

    lax.fori_loop(0, (side_count + side_group - 1) // side_group, side_blocks, 0)


def pull_kernel(
    members, zp, zs, sliced, stash, atoms_ref, near_target, far_target, target_ref, rho, *rest
):
    if stash:
        gy, slope, *rest = rest
        mean_ref, *outs, grad, wanted, mean_vmem, pulled, rows, forces, pull_list, sems = rest
    else:
        mean_ref, *outs, grad, wanted, mean_vmem, pulled, rows, forces, pull_list, sems, gy, slope = rest
    odd = lax.rem(lax.axis_index("sx"), 2)
    if sliced:
        z_first = pl.multiple_of(lax.axis_index("replica") * zs, 8)
        source = target_ref.at[:, pl.ds(z_first, zs), :]
    else:
        source = target_ref
    fetches = [
        pltpu.make_async_copy(source, wanted.at[pl.ds(REACH, CX)], sems.at[0]),
        pltpu.make_async_copy(
            near_target, wanted.at[pl.ds((REACH + CX) * (1 - odd), REACH)], sems.at[1]
        ),
        pltpu.make_async_copy(far_target, wanted.at[pl.ds((REACH + CX) * odd, REACH)], sems.at[2]),
    ]
    for fetch in fetches:
        fetch.start()

    def list_member(member, count):
        return listed(pull_list, count, 0, 1, member * BLOCKS, live_of(atoms_ref, member))

    pull_count = lax.fori_loop(0, members, list_member, jnp.int32(0), unroll=members <= 4)
    forces[...] = jnp.zeros_like(forces)
    grad[:, :, NY - 96 :] = jnp.zeros((members, SPAN * zp, LANES - NY + 96), jnp.bfloat16)
    if not stash:
        zero_tails(gy, slope)
    tables = Tables(zp, zs, atoms_ref)

    for fetch in fetches:
        fetch.wait()

    group = max(1, 16 // zp)

    def gradient(t, carry):
        at = pl.ds(pl.multiple_of(t * group * zp, 16), group * zp)
        planes = pl.ds(t * group, group)
        here = [rho[m, at, 0:NY] for m in range(members)]
        first = functools.reduce(jnp.add, here)
        second = functools.reduce(jnp.add, [f * f for f in here])
        mean = first * (1.0 / members)
        spread = second * (1.0 / members) - mean * mean
        noise = noise_floor + spread * (1.0 / members)
        guess = pl.reciprocal(noise, approx=True)
        inv = guess * (2.0 - noise * guess)
        pull = (wanted[planes].reshape(group * zp, NY) - mean) * inv
        gain = (inv - pull * pull) * (1.0 / (members * members))
        offset = pull * (-1.0 / members) - gain * mean
        for m in range(members):
            grad[m, at, 0:NY] = (offset + gain * here[m]).astype(jnp.bfloat16)
        mean_vmem[planes] = mean.reshape(group, zp, NY)
        return carry

    lax.fori_loop(0, SPAN // group, gradient, 0)
    give = pltpu.make_async_copy(mean_vmem.at[pl.ds(REACH, CX)], mean_ref, sems.at[3])
    give.start()

    def pull_pair(pair, carry):
        for part in range(2):
            code = pull_list[jnp.minimum(2 * pair + part, pull_count - 1)]
            member, block = code // BLOCKS, lax.rem(code, BLOCKS)
            frac_x, frac_y, frac_z, q, power, weight = tables.own_fields(member, block)
            gx, off_x = tables.x(frac_x, power, REACH, 0, SPAN, True)
            gz, off_z = tables.z(frac_z, power)
            rows[part, 0:SPAN] = gx
            rows[part, SPAN : 2 * SPAN] = gx * off_x * q
            slot = code if stash else part
            if not stash:
                tables.y(gy.at[slot], slope.at[slot], frac_y, power, q)
            pulled[part] = jnp.dot(
                grad[member], jnp.concatenate([gy[slot], slope[slot]], 1),
                preferred_element_type=jnp.float32,
            )
            sum_x = jnp.zeros((zp, BLOCK), jnp.float32)
            sum_y = jnp.zeros((zp, BLOCK), jnp.float32)
            sum_z = jnp.zeros((zp, BLOCK), jnp.float32)
            for t in range(SPAN):
                plain = pulled[part, t * zp : (t + 1) * zp, 0:BLOCK]
                slanted = pulled[part, t * zp : (t + 1) * zp, BLOCK:]
                here = rows[part, t : t + 1]
                sum_x += rows[part, SPAN + t : SPAN + t + 1] * plain
                sum_y += here * slanted
                sum_z += here * plain
            at = pl.ds(block, 1)
            forces[member, 0, at] = weight * jnp.sum(sum_x * gz, 0, keepdims=True)
            forces[member, 1, at] = weight * jnp.sum(sum_y * gz, 0, keepdims=True)
            forces[member, 2, at] = weight * jnp.sum(sum_z * (gz * off_z * q), 0, keepdims=True)
        return carry

    lax.fori_loop(0, (pull_count + 1) // 2, pull_pair, 0)
    if len(outs) == 1:
        outs[0][...] = forces[...]
    else:
        for m, out in enumerate(outs):
            out[...] = forces[m]
    give.wait()


def shards(coords, widths, amplitudes, live_blocks, target_map):
    members = lax.axis_size("replica")
    bricks = lax.axis_size("sx")
    rank = lax.axis_index("replica")
    zs = NZ // members
    zp = max(zs, 8)
    sliced = zs % 8 == 0
    few = members <= 4 and members & (members - 1) == 0
    stash = members <= STASH_LIMIT
    blocks = (BLOCKS, BLOCK)
    vmem = pl.BlockSpec(memory_space=pltpu.VMEM)
    anywhere = pl.BlockSpec(memory_space=pl.ANY)

    target = target_map
    if not sliced:
        part = lax.dynamic_slice_in_dim(target_map, rank * zs, zs, 1)
        target = jnp.pad(part, ((0, 0), (0, zp - zs), (0, 0)))
    alive = lax.broadcasted_iota(jnp.int32, (1,) + blocks, 1) < live_blocks[0, 0]
    weights = jnp.where(alive, amplitudes.reshape((1,) + blocks), 0.0)
    own = jnp.concatenate([coords.reshape((3,) + blocks), widths.reshape((1,) + blocks), weights])

    odd = lax.rem(lax.axis_index("sx"), 2)

    def edge(plane):
        z_first = rank * zs if sliced else 0
        return lax.dynamic_slice(target, (plane, z_first, 0), (REACH, zp, NY))

    near_edge, far_edge = edge((CX - REACH) * (1 - odd)), edge((CX - REACH) * odd)

    def swap(block, pairs):
        return lax.ppermute(block, "sx", pairs + [(b, a) for a, b in pairs])

    near_pairs = [(i, i + 1) for i in range(0, bricks - 1, 2)]
    far_pairs = [(i, i + 1) for i in range(1, bricks - 1, 2)]

    def across(block, k):
        return lax.ppermute(block, "replica", [(i, i ^ k) for i in range(members)])

    if few:
        everyone = jnp.stack([own] + [across(own, k) for k in range(1, members)])
    else:
        everyone = lax.all_gather(own, "replica")
    far, near = swap(everyone, far_pairs), swap(everyone, near_pairs)
    near_edge, far_edge, _ = lax.optimization_barrier((near_edge, far_edge, everyone))
    far_target, near_target = swap(far_edge, far_pairs), swap(near_edge, near_pairs)

    force_shapes = (
        [jax.ShapeDtypeStruct((3,) + blocks, jnp.float32)] * members
        if few
        else [jax.ShapeDtypeStruct((members, 3) + blocks, jnp.float32)]
    )
    table = ((members * BLOCKS if stash else 4), LANES, BLOCK)
    tables = [jax.ShapeDtypeStruct(table, jnp.bfloat16)] * 2 if stash else []
    splat = pl.pallas_call(
        functools.partial(splat_kernel, members, zp, zs, stash),
        out_shape=[jax.ShapeDtypeStruct((members, SPAN * zp, LANES), jnp.float32)] + tables,
        in_specs=[vmem] * 3,
        out_specs=[vmem] * (1 + len(tables)),
        scratch_shapes=([] if stash else [pltpu.VMEM(table, jnp.bfloat16)])
        + [
            pltpu.VMEM((4, LANES, BLOCK), jnp.bfloat16),
            pltpu.VMEM((2, members, FIELDS) + blocks, jnp.float32),
            pltpu.VMEM((4, SPAN * zp, BLOCK), jnp.bfloat16),
            pltpu.VMEM((4, LAP * zp, BLOCK), jnp.bfloat16),
            pltpu.VMEM((4, SPAN, BLOCK), jnp.float32),
            pltpu.SMEM((members * BLOCKS + 1,), jnp.int32),
            pltpu.SMEM((2 * members * BLOCKS + 1,), jnp.int32),
        ],
        compiler_params=pltpu.CompilerParams(vmem_limit_bytes=24 * 1024 * 1024),
        cost_estimate=pl.CostEstimate(flops=6_000_000_000, bytes_accessed=14_000_000, transcendentals=0),
        name="splat",
    )(everyone, near, far)
    mean, *partial = pl.pallas_call(
        functools.partial(pull_kernel, members, zp, zs, sliced, stash),
        out_shape=[jax.ShapeDtypeStruct((CX, zp, NY), jnp.float32)] + force_shapes,
        in_specs=[vmem, anywhere, anywhere, anywhere] + [vmem] * len(splat),
        out_specs=[anywhere] + [vmem] * len(force_shapes),
        scratch_shapes=[
            pltpu.VMEM((members, SPAN * zp, LANES), jnp.bfloat16),
            pltpu.VMEM((SPAN, zp, NY), jnp.float32),
            pltpu.VMEM((SPAN, zp, NY), jnp.float32),
            pltpu.VMEM((2, SPAN * zp, 2 * BLOCK), jnp.float32),
            pltpu.VMEM((2, 2 * SPAN, BLOCK), jnp.float32),
            pltpu.VMEM((members, 3) + blocks, jnp.float32),
            pltpu.SMEM((members * BLOCKS + 1,), jnp.int32),
            pltpu.SemaphoreType.DMA((4,)),
        ]
        + ([] if stash else [pltpu.VMEM(table, jnp.bfloat16)] * 2),
        compiler_params=pltpu.CompilerParams(vmem_limit_bytes=(24 if stash else 40) * 1024 * 1024),
        cost_estimate=pl.CostEstimate(flops=6_000_000_000, bytes_accessed=14_000_000, transcendentals=0),
        name="pull",
    )(everyone, near_target, far_target, target, *splat)

    if few:
        forces = partial[0]
        for k in range(1, members):
            forces = forces + across(partial[k], k)
    else:
        forces = lax.psum_scatter(partial[0], "replica", scatter_dimension=0)
    return mean[:, :zs], forces.reshape(3, 1, ATOMS_DEV)


def solution(mesh):
    placed = (
        P(None, ("groups", "replica"), "sx"),
        P(("groups", "replica"), "sx"),
        P(("groups", "replica"), "sx"),
        P(("groups", "replica"), "sx"),
        P(("groups", "sx"), None, None),
    )
    return jax.shard_map(
        shards,
        mesh=mesh,
        in_specs=placed,
        out_specs=(P(("groups", "sx"), "replica", None), P(None, ("groups", "replica"), "sx")),
        check_vma=False,
    )
```

time: 45.9 us -> 38.6 us (0.84)
  the two profiles are of different devices: /device:TPU:1 before, /device:TPU:0 now
where the time goes in v1:
time: 38.6 us; the launch traced here: 38.5 us
  starting transfers between devices  14.5 us (38%)
  Pallas kernels  12 us (31%)
  waiting for transfers between devices  7.47 us (19%)
  other arithmetic  2.1 us (5%)
  between operations  1.39 us (4%)
  local copies, waits for them, and re-layouts  1.05 us (3%)
    ppermute x6, starting transfers between devices, across(): return lax.ppermute(block, 'replica', [(i, i ^ k) for i in range(members)])  10.1 us
    ppermute x6, waiting for transfers between devices, across(): return lax.ppermute(block, 'replica', [(i, i ^ k) for i in range(members)])  7.46 us
    pallas_call x1, Pallas kernels, shards(): pl.pallas_call(functools.partial(pull_kernel, members, zp, zs, sliced, st...  6.46 us
    pallas_call x1, Pallas kernels, shards(): pl.pallas_call(functools.partial(splat_kernel, members, zp, zs, stash), o...  5.53 us
    ppermute x4, starting transfers between devices, swap(): return lax.ppermute(block, 'sx', pairs + [(b, a) for a, b in pairs])  4.46 us
    dynamic_slice x1, local copies, waits for them, and re-layouts, edge(): return lax.dynamic_slice(target, (plane, z_first, 0), (REACH, zp, NY))  1.05 us
  transfers between devices with their start and end apart: 10, of which 5 were waited for; matrix products, arithmetic and copies ran while one was open for 3% of the time, Pallas kernels for 14%

profile of v1, /device:TPU:0, one launch (start us, length us, event | category | flops | bytes accessed | tf_op | source)
XLA Modules:
  0.0 38.5 jit_solution(9556586608650569843)
XLA Ops:
  1.3 0.8 %broadcast_select_fusion = f32[1,8,128]{2,1,0:T(8,128)S(1)} fusion(f32[1,8,128]{2,1,0:T(8,128)} %bitcast.16, pred[8]{0:T(512)(128)(4,1)S(1)} %iota_compare_fusion), kind=kLoop, calls=%fused_computation.3 | loop fusion | flops 1024 | bytes 8200 | tf_op jit(solution)/shard_map/jit(_where)/select_n | solution.py:305
  2.0 0.7 %fusion = (f32[1,5,8,128]{3,2,1,0:T(8,128)S(1)}, f32[5,8,128]{2,1,0:T(8,128)S(1)}) fusion(f32[1,8,128]{2,1,0:T(8,128)S(1)} %broadcast_select_fusion, f32[1,8,128]{2,1,0:T(8,128)} %bitcast.17, f32[3,8,128]{2,1,0:T(8,128)} %bitcast.14), kind=kLoop, calls=%fused_computation.7 | loop fusion | flops 10240 | bytes 61440 | tf_op jit(solution)/shard_map/stack | solution.py:326
  2.8 4.0 %collective-permute-start.1 = (f32[5,8,128]{2,1,0:T(8,128)S(1)}, f32[5,8,128]{2,1,0:T(8,128)S(1)}, u32[]{:S(2)}, u32[]{:S(2)}) collective-permute-start(f32[5,8,128]{2,1,0:T(8,128)S(1)} %get-tuple-element.29), channel_id=1, source_target_pairs={{0,8},{4,12},{8,0},{12,4},{1,9},{5,13},{9,1},{13,5},{2,10},{6,14},... | collective-permute-start | bytes 61448 | tf_op jit(solution)/shard_map/ppermute | solution.py:323
  6.8 1.6 %collective-permute-start = (f32[5,8,128]{2,1,0:T(8,128)S(1)}, f32[5,8,128]{2,1,0:T(8,128)S(1)}, u32[]{:S(2)}, u32[]{:S(2)}) collective-permute-start(f32[5,8,128]{2,1,0:T(8,128)S(1)} %get-tuple-element.29), channel_id=1, source_target_pairs={{0,4},{4,0},{8,12},{12,8},{1,5},{5,1},{9,13},{13,9},{2,6},{6,2},{1... | collective-permute-start | bytes 61448 | tf_op jit(solution)/shard_map/ppermute | solution.py:323
  8.4 0.0 collective-permute-start.2
  8.4 0.2 collective-permute-done.1
  8.6 2.0 %collective-permute-done = f32[5,8,128]{2,1,0:T(8,128)S(1)} collective-permute-done((f32[5,8,128]{2,1,0:T(8,128)S(1)}, f32[5,8,128]{2,1,0:T(8,128)S(1)}, u32[]{:S(2)}, u32[]{:S(2)}) %collective-permute-start) | collective-permute-done | bytes 20512 | tf_op jit(solution)/shard_map/ppermute | solution.py:323
  10.6 3.4 %collective-permute-done.2 = f32[5,8,128]{2,1,0:T(8,128)S(1)} collective-permute-done((f32[5,8,128]{2,1,0:T(8,128)S(1)}, f32[5,8,128]{2,1,0:T(8,128)S(1)}, u32[]{:S(2)}, u32[]{:S(2)}) %collective-permute-start.2) | collective-permute-done | bytes 20512 | tf_op jit(solution)/shard_map/ppermute | solution.py:323
  14.0 0.7 %collective-permute-start.6 = (f32[4,5,8,128]{3,2,1,0:T(8,128)S(1)}, f32[4,5,8,128]{3,2,1,0:T(8,128)S(1)}, u32[]{:S(2)}, u32[]{:S(2)}) collective-permute-start(f32[4,5,8,128]{3,2,1,0:T(8,128)S(1)} %pad_maximum_fusion.atoms_ref), channel_id=1, source_target_pairs={{1,2},{2,1},{5,6},{6,5},{9,10},{10,9},{13,14},{14,13},{17,18},{18,... | collective-permute-start | bytes 245768 | tf_op jit(solution)/shard_map/ppermute | solution.py:317
  14.6 2.9 %collective-permute-start.5 = (f32[4,5,8,128]{3,2,1,0:T(8,128)S(1)}, f32[4,5,8,128]{3,2,1,0:T(8,128)S(1)}, u32[]{:S(2)}, u32[]{:S(2)}) collective-permute-start(f32[4,5,8,128]{3,2,1,0:T(8,128)S(1)} %pad_maximum_fusion.atoms_ref), channel_id=1, source_target_pairs={{0,1},{2,3},{1,0},{3,2},{4,5},{6,7},{5,4},{7,6},{8,9},{10,11},{9,8... | collective-permute-start | bytes 245768 | tf_op jit(solution)/shard_map/ppermute | solution.py:317
  17.6 1.0 %constant_dynamic-slice_fusion = (f32[6,16,480]{2,1,0:T(8,128)S(1)}, f32[6,16,480]{2,1,0:T(8,128)S(1)}) fusion(f32[24,64,480]{2,1,0:T(8,128)} %target_ref.1, s32[]{:T(128)S(6)} %select_n.25, s32[]{:T(128)S(6)} %select_n.24, s32[]{:T(128)S(6)} %select_n.23), kind=kLoop, calls=%fused_computation.4 | loop fusion | bytes 737292 | tf_op jit(solution)/shard_map/dynamic_slice | solution.py:312
  18.6 0.0 copy-start
  18.6 0.1 collective-permute-start.3
  18.7 0.8 %collective-permute-start.4 = (f32[6,16,480]{2,1,0:T(8,128)S(1)}, f32[6,16,480]{2,1,0:T(8,128)S(1)}, u32[]{:S(2)}, u32[]{:S(2)}) collective-permute-start(f32[6,16,480]{2,1,0:T(8,128)S(1)} %get-tuple-element.13), channel_id=1, source_target_pairs={{1,2},{2,1},{5,6},{6,5},{9,10},{10,9},{13,14},{14,13},{17,18},{18,... | collective-permute-start | bytes 552968 | tf_op jit(solution)/shard_map/ppermute | solution.py:317
  19.5 0.0 collective-permute-done.6.far_ref
  19.5 0.0 collective-permute-done.5.near_ref
  19.5 5.5 %splat.1 = (f32[4,576,512]{2,1,0:T(8,128)S(1)}, bf16[32,512,128]{2,1,0:T(8,128)(2,1)S(1)}, bf16[32,512,128]{2,1,0:T(8,128)(2,1)S(1)}) custom-call(f32[4,5,8,128]{3,2,1,0:T(8,128)S(1)} %pad_maximum_fusion.atoms_ref, f32[4,5,8,128]{3,2,1,0:T(8,128)S(1)} %collective-permute-done.5.near_ref, f32[4,5,8,128]{3,2,1,0:T(8,128)S(1)} %collective-permute-done.6.far_ref), custom_call_target="tpu_custom_call" | custom-call | flops 6000000000 | bytes 14000000 | tf_op jit(solution)/shard_map/splat/pallas_call | solution.py:340
  25.1 0.0 collective-permute-done.3.near_target
  25.1 0.0 collective-permute-done.4.far_target
  25.1 0.0 copy-done
  25.1 6.5 %pull.1 = (f32[24,16,480]{2,1,0:T(8,128)}, f32[3,8,128]{2,1,0:T(8,128)S(1)}, f32[3,8,128]{2,1,0:T(8,128)S(1)}, f32[3,8,128]{2,1,0:T(8,128)S(1)}, f32[3,8,128]{2,1,0:T(8,128)S(1)}) custom-call(f32[4,5,8,128]{3,2,1,0:T(8,128)S(1)} %pad_maximum_fusion.atoms_ref, f32[6,16,480]{2,1,0:T(8,128)S(1)} %collective-permute-done.3.near_target, ...), custom_call_target="tpu_custom_call" | custom-call | flops 6000000000 | bytes 14000000 | tf_op jit(solution)/shard_map/pull/pallas_call | solution.py:359
  31.6 0.1 collective-permute-start.7
  31.7 0.8 %collective-permute-start.8 = (f32[3,8,128]{2,1,0:T(8,128)S(1)}, f32[3,8,128]{2,1,0:T(8,128)S(1)}, u32[]{:S(2)}, u32[]{:S(2)}) collective-permute-start(f32[3,8,128]{2,1,0:T(8,128)S(1)} %get-tuple-element.20), channel_id=1, source_target_pairs={{0,8},{4,12},{8,0},{12,4},{1,9},{5,13},{9,1},{13,5},{2,10},{6,14},... | collective-permute-start | bytes 36872 | tf_op jit(solution)/shard_map/ppermute | solution.py:323
  32.4 3.6 %collective-permute-start.9 = (f32[3,8,128]{2,1,0:T(8,128)S(1)}, f32[3,8,128]{2,1,0:T(8,128)S(1)}, u32[]{:S(2)}, u32[]{:S(2)}) collective-permute-start(f32[3,8,128]{2,1,0:T(8,128)S(1)} %get-tuple-element.21), channel_id=1, source_target_pairs={{0,12},{4,8},{8,4},{12,0},{1,13},{5,9},{9,5},{13,1},{2,14},{6,10},... | collective-permute-start | bytes 36872 | tf_op jit(solution)/shard_map/ppermute | solution.py:323
  36.0 0.0 collective-permute-done.7
  36.0 0.4 %collective-permute-done.8 = f32[3,8,128]{2,1,0:T(8,128)S(1)} collective-permute-done((f32[3,8,128]{2,1,0:T(8,128)S(1)}, f32[3,8,128]{2,1,0:T(8,128)S(1)}, u32[]{:S(2)}, u32[]{:S(2)}) %collective-permute-start.8) | collective-permute-done | bytes 12320 | tf_op jit(solution)/shard_map/ppermute | solution.py:323
  36.5 1.4 %collective-permute-done.9 = f32[3,8,128]{2,1,0:T(8,128)S(1)} collective-permute-done((f32[3,8,128]{2,1,0:T(8,128)S(1)}, f32[3,8,128]{2,1,0:T(8,128)S(1)}, u32[]{:S(2)}, u32[]{:S(2)}) %collective-permute-start.9) | collective-permute-done | bytes 12320 | tf_op jit(solution)/shard_map/ppermute | solution.py:323
  37.9 0.6 %add_add_fusion = f32[3,8,128]{2,1,0:T(8,128)} fusion(f32[3,8,128]{2,1,0:T(8,128)S(1)} %collective-permute-done.9, f32[3,8,128]{2,1,0:T(8,128)S(1)} %collective-permute-done.8, f32[3,8,128]{2,1,0:T(8,128)S(1)} %get-tuple-element.18, f32[3,8,128]{2,1,0:T(8,128)S(1)} %collective-permute-done.7), kind=kLoop, calls=%fused_computation.2 | loop fusion | flops 9216 | bytes 61440 | tf_op jit(solution)/shard_map/add | solution.py:383
  (2 shorter events, 0.0 us)
Async XLA Ops:
  2.8 5.8 %collective-permute-start.1 = (f32[5,8,128]{2,1,0:T(8,128)S(1)}, f32[5,8,128]{2,1,0:T(8,128)S(1)}, u32[]{:S(2)}, u32[]{:S(2)}) collective-permute-start(f32[5,8,128]{2,1,0:T(8,128)S(1)} %get-tuple-element.29), channel_id=1, source_target_pairs={{0,8},{4,12},{8,0},{12,4},{1,9},{5,13},{9,1},{13,5},{2,10},{6,14},... | collective-permute-start | bytes 61448 | tf_op jit(solution)/shard_map/ppermute | solution.py:323
  6.8 3.8 %collective-permute-start = (f32[5,8,128]{2,1,0:T(8,128)S(1)}, f32[5,8,128]{2,1,0:T(8,128)S(1)}, u32[]{:S(2)}, u32[]{:S(2)}) collective-permute-start(f32[5,8,128]{2,1,0:T(8,128)S(1)} %get-tuple-element.29), channel_id=1, source_target_pairs={{0,4},{4,0},{8,12},{12,8},{1,5},{5,1},{9,13},{13,9},{2,6},{6,2},{1... | collective-permute-start | bytes 61448 | tf_op jit(solution)/shard_map/ppermute | solution.py:323
  8.4 5.6 %collective-permute-start.2 = (f32[5,8,128]{2,1,0:T(8,128)S(1)}, f32[5,8,128]{2,1,0:T(8,128)S(1)}, u32[]{:S(2)}, u32[]{:S(2)}) collective-permute-start(f32[5,8,128]{2,1,0:T(8,128)S(1)} %get-tuple-element.29), channel_id=1, source_target_pairs={{0,12},{4,8},{8,4},{12,0},{1,13},{5,9},{9,5},{13,1},{2,14},{6,10},... | collective-permute-start | bytes 61448 | tf_op jit(solution)/shard_map/ppermute | solution.py:323
  14.0 5.5 %collective-permute-start.6 = (f32[4,5,8,128]{3,2,1,0:T(8,128)S(1)}, f32[4,5,8,128]{3,2,1,0:T(8,128)S(1)}, u32[]{:S(2)}, u32[]{:S(2)}) collective-permute-start(f32[4,5,8,128]{3,2,1,0:T(8,128)S(1)} %pad_maximum_fusion.atoms_ref), channel_id=1, source_target_pairs={{1,2},{2,1},{5,6},{6,5},{9,10},{10,9},{13,14},{14,13},{17,18},{18,... | collective-permute-start | bytes 245768 | tf_op jit(solution)/shard_map/ppermute | solution.py:317
  14.6 4.9 %collective-permute-start.5 = (f32[4,5,8,128]{3,2,1,0:T(8,128)S(1)}, f32[4,5,8,128]{3,2,1,0:T(8,128)S(1)}, u32[]{:S(2)}, u32[]{:S(2)}) collective-permute-start(f32[4,5,8,128]{3,2,1,0:T(8,128)S(1)} %pad_maximum_fusion.atoms_ref), channel_id=1, source_target_pairs={{0,1},{2,3},{1,0},{3,2},{4,5},{6,7},{5,4},{7,6},{8,9},{10,11},{9,8... | collective-permute-start | bytes 245768 | tf_op jit(solution)/shard_map/ppermute | solution.py:317
  18.6 6.5 %copy-start = (f32[24,64,480]{2,1,0:T(8,128)S(1)}, f32[24,64,480]{2,1,0:T(8,128)}, u32[]{:S(2)}) copy-start(f32[24,64,480]{2,1,0:T(8,128)} %target_ref.1) | copy-start | bytes 8847364
  18.6 6.5 %collective-permute-start.3 = (f32[6,16,480]{2,1,0:T(8,128)S(1)}, f32[6,16,480]{2,1,0:T(8,128)S(1)}, u32[]{:S(2)}, u32[]{:S(2)}) collective-permute-start(f32[6,16,480]{2,1,0:T(8,128)S(1)} %get-tuple-element.12), channel_id=1, source_target_pairs={{0,1},{2,3},{1,0},{3,2},{4,5},{6,7},{5,4},{7,6},{8,9},{10,11},{9,8... | collective-permute-start | bytes 552968 | tf_op jit(solution)/shard_map/ppermute | solution.py:317
  18.7 6.4 %collective-permute-start.4 = (f32[6,16,480]{2,1,0:T(8,128)S(1)}, f32[6,16,480]{2,1,0:T(8,128)S(1)}, u32[]{:S(2)}, u32[]{:S(2)}) collective-permute-start(f32[6,16,480]{2,1,0:T(8,128)S(1)} %get-tuple-element.13), channel_id=1, source_target_pairs={{1,2},{2,1},{5,6},{6,5},{9,10},{10,9},{13,14},{14,13},{17,18},{18,... | collective-permute-start | bytes 552968 | tf_op jit(solution)/shard_map/ppermute | solution.py:317
  31.6 4.5 %collective-permute-start.7 = (f32[3,8,128]{2,1,0:T(8,128)S(1)}, f32[3,8,128]{2,1,0:T(8,128)S(1)}, u32[]{:S(2)}, u32[]{:S(2)}) collective-permute-start(f32[3,8,128]{2,1,0:T(8,128)S(1)} %get-tuple-element.19), channel_id=1, source_target_pairs={{0,4},{4,0},{8,12},{12,8},{1,5},{5,1},{9,13},{13,9},{2,6},{6,2},{1... | collective-permute-start | bytes 36872 | tf_op jit(solution)/shard_map/ppermute | solution.py:323
  31.7 4.8 %collective-permute-start.8 = (f32[3,8,128]{2,1,0:T(8,128)S(1)}, f32[3,8,128]{2,1,0:T(8,128)S(1)}, u32[]{:S(2)}, u32[]{:S(2)}) collective-permute-start(f32[3,8,128]{2,1,0:T(8,128)S(1)} %get-tuple-element.20), channel_id=1, source_target_pairs={{0,8},{4,12},{8,0},{12,4},{1,9},{5,13},{9,1},{13,5},{2,10},{6,14},... | collective-permute-start | bytes 36872 | tf_op jit(solution)/shard_map/ppermute | solution.py:323
  32.4 5.5 %collective-permute-start.9 = (f32[3,8,128]{2,1,0:T(8,128)S(1)}, f32[3,8,128]{2,1,0:T(8,128)S(1)}, u32[]{:S(2)}, u32[]{:S(2)}) collective-permute-start(f32[3,8,128]{2,1,0:T(8,128)S(1)} %get-tuple-element.21), channel_id=1, source_target_pairs={{0,12},{4,8},{8,4},{12,0},{1,13},{5,9},{9,5},{13,1},{2,14},{6,10},... | collective-permute-start | bytes 36872 | tf_op jit(solution)/shard_map/ppermute | solution.py:323
